TPU v7x, 256 devices: a whole 4x4x8 slice. The times are simulated.
256 devices in a mesh: seq: 32 (over z_lo, x, core), dp: 8 (over y, z_hi).
Axes of the slice: x: 4, y: 4, z: 8 (z_hi: 2, z_lo: 4; z = z_hi * 4 + z_lo), core: 2. Of those that a mesh axis runs over, the one named last changes fastest.
Arguments:
- features: bfloat16 [64, 4096, 768], P('dp', 'seq'), may hold values from -6 to 6
- kernel: bfloat16 [3, 768, 768], replicated, may hold values from -0.125 to 0.125
- cotangent: bfloat16 [64, 4096, 768], P('dp', 'seq'), may hold values from -6 to 6
Outputs:
- outputs: bfloat16 [64, 4096, 768], P('dp', 'seq')
- input_grad: bfloat16 [64, 4096, 768], P('dp', 'seq')
- weight_grad: float32 [3, 768, 768], P(None, 'seq', 'dp')
All inputs are finite; a program needn't handle non-finite values.
Results may differ from a plain program's by a relative error of at most 0.0034.
Values may be sent and summed in bfloat16 or wider, within the bound.
A program may use at most 64 MiB of HBM per device.

v0:
```python
import math

import jax
import jax.numpy as jnp
from jax import lax
from jax.sharding import PartitionSpec as P


def padded(cells, sides, width):
    for axis, dim in sides:
        count = lax.axis_size(axis)
        ends = count - 1
        head = lax.slice_in_dim(cells, 0, width, axis=dim)
        tail = lax.slice_in_dim(cells, cells.shape[dim] - width, cells.shape[dim], axis=dim)
        cells = jnp.concatenate(
            [
                lax.ppermute(tail, axis, [(i, (i + 1) % count) for i in range(ends)]),
                cells,
                lax.ppermute(head, axis, [((i + 1) % count, i) for i in range(ends)]),
            ],
            axis=dim,
        )
    return cells


def on_device(features, kernel, cotangent):
    seqs_here, bins_here, width = features.shape
    spread = bins_here // 2
    widened = features.astype(jnp.float32)
    gelu_output = jax.nn.gelu(widened).astype(jnp.bfloat16)
    act_wide = padded(gelu_output, (("seq", 1),), spread)
    up_wide = padded(cotangent, (("seq", 1),), spread)
    act_taps = [
        act_wide[:, kernel_tap_index * spread : kernel_tap_index * spread + bins_here]
        for kernel_tap_index in range(3)
    ]
    up_taps = [
        up_wide[:, (2 - kernel_tap_index) * spread : (2 - kernel_tap_index) * spread + bins_here]
        for kernel_tap_index in range(3)
    ]
    conv_sum = jnp.einsum("stc,cd->std", act_taps[0], kernel[0], preferred_element_type=jnp.float32)
    back_sum = jnp.einsum("std,cd->stc", up_taps[0], kernel[0], preferred_element_type=jnp.float32)
    for kernel_tap_index in range(1, 3):
        conv_sum = conv_sum + jnp.einsum(
            "stc,cd->std",
            act_taps[kernel_tap_index],
            kernel[kernel_tap_index],
            preferred_element_type=jnp.float32,
        )
        back_sum = back_sum + jnp.einsum(
            "std,cd->stc",
            up_taps[kernel_tap_index],
            kernel[kernel_tap_index],
            preferred_element_type=jnp.float32,
        )
    outputs = (widened + conv_sum).astype(jnp.bfloat16)
    unused, pullback = jax.vjp(jax.nn.gelu, widened)
    slope_term = pullback(back_sum)[0]
    input_grad = (cotangent.astype(jnp.float32) + slope_term).astype(jnp.bfloat16)
    seq_count = lax.axis_size("seq")
    dp_count = lax.axis_size("dp")
    partial_terms = jnp.stack(
        [
            jnp.einsum(
                "stc,std->cd",
                act_taps[kernel_tap_index],
                cotangent,
                preferred_element_type=jnp.float32,
            )
            for kernel_tap_index in range(3)
        ],
        axis=0,
    )
    by_bins = lax.psum_scatter(partial_terms, "seq", scatter_dimension=1, tiled=True)
    summed = lax.psum_scatter(by_bins, "dp", scatter_dimension=2, tiled=True)
    factor = 1.0 / math.sqrt(seqs_here * bins_here * seq_count * dp_count)
    return (outputs, input_grad, summed * factor)


def solution(mesh):
    in_specs = (P("dp", "seq", None), P(), P("dp", "seq", None))
    out_specs = (P("dp", "seq", None), P("dp", "seq", None), P(None, "seq", "dp"))
    return jax.shard_map(
        on_device, mesh=mesh, in_specs=in_specs, out_specs=out_specs, check_vma=False
    )
```

profile of v0, /device:TPU:1, one launch (start us, length us, event | category | flops | bytes accessed | tf_op | source)
XLA Modules:
  0.0 284.3 jit_solution(15967416358197026205)
XLA Ops:
  7.2 2.6 fusion.8
  10.0 5.1 %collective-permute-start.1 = (bf16[8,64,768]{2,1,0:T(8,128)(2,1)S(1)}, bf16[8,64,768]{2,1,0:T(8,128)(2,1)S(1)}, u32[]{:S(2)}, u32[]{:S(2)}) collective-permute-start(bf16[8,64,768]{2,1,0:T(8,128)(2,1)S(1)} %get-tuple-element.5), channel_id=1, source_target_pairs={{8,0},{16,8},{24,16},{32,24},{40,32},{48,40},{56,48},{64,56},{72,6... | collective-permute-start | bytes 2359304 | tf_op jit(solution)/shard_map/ppermute | solution.py:19
  15.2 1.9 collective-permute-start
  17.1 1.9 convolution_bitcast_fusion.1
  19.0 5.1 %collective-permute-done.1 = bf16[8,64,768]{2,1,0:T(8,128)(2,1)S(1)} collective-permute-done((bf16[8,64,768]{2,1,0:T(8,128)(2,1)S(1)}, bf16[8,64,768]{2,1,0:T(8,128)(2,1)S(1)}, u32[]{:S(2)}, u32[]{:S(2)}) %collective-permute-start.1) | collective-permute-done | bytes 786464 | tf_op jit(solution)/shard_map/ppermute | solution.py:19
  24.2 1.5 convolution_bitcast_fusion
  26.0 0.9 copy-done.5
  26.9 1.5 convolution_bitcast_fusion.2
  28.3 3.4 %pad_maximum_fusion = f32[3,768,768]{2,1,0:T(8,128)} fusion(f32[1,768,768]{2,1,0:T(8,128)S(1)} %convolution_bitcast_fusion, f32[1,768,768]{2,1,0:T(8,128)S(1)} %convolution_bitcast_fusion.1, f32[1,768,768]{2,1,0:T(8,128)S(1)} %convolution_bitcast_fusion.2), kind=kLoop, calls=%fused_computation | loop fusion | flops 3538944 | bytes 14155776 | tf_op jit(solution)/shard_map/stack | solution.py:62
  31.8 1.5 fusion.42
  33.3 1.9 collective-permute-start.2
  35.2 4.8 %collective-permute-start.3 = (bf16[8,64,768]{2,1,0:T(8,128)(2,1)S(1)}, bf16[8,64,768]{2,1,0:T(8,128)(2,1)S(1)}, u32[]{:S(2)}, u32[]{:S(2)}) collective-permute-start(bf16[8,64,768]{2,1,0:T(8,128)(2,1)S(1)} %get-tuple-element.3), channel_id=1, source_target_pairs={{0,8},{8,16},{16,24},{24,32},{32,40},{40,48},{48,56},{56,64},{64,7... | collective-permute-start | bytes 2359304 | tf_op jit(solution)/shard_map/ppermute | solution.py:17
  40.1 5.1 %fusion.21 = f32[8,128,768]{2,1,0:T(8,128)} fusion(bf16[3,768,768]{2,1,0:T(8,128)(2,1)} %param.4, bf16[8,128,768]{2,1,0:T(8,128)(2,1)S(1)} %copy-done), kind=kOutput, calls=%fused_computation.35 | convolution fusion | flops 1215823872 | bytes 5898240 | tf_op jit(solution)/shard_map/stc,cd->std/dot_general | solution.py:44
  45.2 1.4 fusion.19
  46.6 3.1 %fusion.24 = f32[8,128,768]{2,1,0:T(8,128)} fusion(bf16[3,768,768]{2,1,0:T(8,128)(2,1)S(1)} %copy-done.4, bf16[8,128,768]{2,1,0:T(8,128)(2,1)S(1)} %fusion.8, bf16[8,64,768]{2,1,0:T(8,128)(2,1)S(1)} %copy-done.6), kind=kOutput, calls=%fused_computation.38 | convolution fusion | flops 1211105280 | bytes 6684672 | tf_op jit(solution)/shard_map/stc,cd->std/dot_general | solution.py:41
  49.7 1.4 fusion.14
  51.1 4.4 %fusion.4 = bf16[8,128,768]{2,1,0:T(8,128)(2,1)} fusion(bf16[8,128,768]{2,1,0:T(8,128)(2,1)S(1)} %copy-done, f32[8,128,768]{2,1,0:T(8,128)S(1)} %fusion.14, f32[8,128,768]{2,1,0:T(8,128)S(1)} %fusion.19, bf16[8,128,768]{2,1,0:T(8,128)(2,1)S(1)} %copy-done.2, bf16[8,64,768]{2,1,0:T(8,128)(2,1)S(1)} %collective-permute-done.3, ...), kind=kOutput, calls=%fused_computation.11 | convolution fusion | flops 1230766080 | bytes 14548992 | tf_op jit(solution)/shard_map/std,cd->stc/dot_general | solution.py:50
  55.5 130.9 %reduce-scatter.5.cloned.1.call-done = f32[3,24,768]{2,1,0:T(8,128)} async-done(((f32[3,768,768]{2,1,0:T(8,128)}), f32[3,24,768]{2,1,0:T(8,128)}) %reduce-scatter.5.cloned.1.call-update) | async-done | bytes 221200 | tf_op jit(solution)/shard_map/reduce_scatter | solution.py:74
  186.5 2.3 copy.15
  188.8 2.5 reshape.12
  191.3 6.1 %fusion.9 = bf16[8,128,768]{2,1,0:T(8,128)(2,1)} fusion(bf16[8,128,768]{2,1,0:T(8,128)(2,1)S(1)} %copy-done, f32[8,128,768]{2,1,0:T(8,128)} %fusion.24, f32[8,128,768]{2,1,0:T(8,128)} %fusion.21, bf16[3,768,768]{2,1,0:T(8,128)(2,1)} %param.4, bf16[8,64,768]{2,1,0:T(8,128)(2,1)} %copy-done.3, bf16[8,128,768]{2,1,0:T(8,128)(2,1)S(1)} %fusion.8), kind=kOutput, calls=%fused_computation.16 | convolution fusion | flops 1215037440 | bytes 12976128 | tf_op jit(solution)/shard_map/stc,cd->std/dot_general | solution.py:44
  197.4 78.4 %reduce-scatter.7.cloned.1.call-done = f32[96,72]{1,0:T(8,128)} async-done(((f32[768,72]{1,0:T(8,128)}), f32[96,72]{1,0:T(8,128)}) %reduce-scatter.7.cloned.1.call-update) | async-done | bytes 27664
  275.8 0.9 reshape.13
  276.8 0.6 broadcast_multiply_fusion
  (22 shorter events, 0.7 us)
Async XLA Ops:
  7.2 9.9 %copy-start = (bf16[8,128,768]{2,1,0:T(8,128)(2,1)S(1)}, bf16[8,128,768]{2,1,0:T(8,128)(2,1)}, u32[]{:S(2)}) copy-start(bf16[8,128,768]{2,1,0:T(8,128)(2,1)} %param.3) | copy-start | bytes 4718596
  7.2 179.3 %reduce-scatter.5.cloned.1.call-start = ((), (), s32[]{:S(2)}) async-start(), calls=%async_computation.2 | async-start | bytes 7299072 | tf_op jit(solution)/shard_map/reduce_scatter | solution.py:74
  7.2 9.9 %copy-start.1 = (bf16[8,128,768]{2,1,0:T(8,128)(2,1)S(1)}, bf16[8,128,768]{2,1,0:T(8,128)(2,1)}, u32[]{:S(2)}) copy-start(bf16[8,128,768]{2,1,0:T(8,128)(2,1)} %param.5) | copy-start | bytes 4718596
  10.0 14.2 %collective-permute-start.1 = (bf16[8,64,768]{2,1,0:T(8,128)(2,1)S(1)}, bf16[8,64,768]{2,1,0:T(8,128)(2,1)S(1)}, u32[]{:S(2)}, u32[]{:S(2)}) collective-permute-start(bf16[8,64,768]{2,1,0:T(8,128)(2,1)S(1)} %get-tuple-element.5), channel_id=1, source_target_pairs={{8,0},{16,8},{24,16},{32,24},{40,32},{48,40},{56,48},{64,56},{72,6... | collective-permute-start | bytes 2359304 | tf_op jit(solution)/shard_map/ppermute | solution.py:19
  15.2 10.8 %collective-permute-start = (bf16[8,64,768]{2,1,0:T(8,128)(2,1)S(1)}, bf16[8,64,768]{2,1,0:T(8,128)(2,1)S(1)}, u32[]{:S(2)}, u32[]{:S(2)}) collective-permute-start(bf16[8,64,768]{2,1,0:T(8,128)(2,1)S(1)} %get-tuple-element.6), channel_id=1, source_target_pairs={{0,8},{8,16},{16,24},{24,32},{32,40},{40,48},{48,56},{56,64},{64,7... | collective-permute-start | bytes 2359304 | tf_op jit(solution)/shard_map/ppermute | solution.py:17
  24.2 1.5 copy-start.3
  26.0 0.9 copy-start.5
  31.7 244.1 %reduce-scatter.7.cloned.1.call-start = ((), (), s32[]{:S(2)}) async-start(), calls=%async_computation.3 | async-start | bytes 442368
  33.3 16.4 %collective-permute-start.2 = (bf16[8,64,768]{2,1,0:T(8,128)(2,1)S(1)}, bf16[8,64,768]{2,1,0:T(8,128)(2,1)S(1)}, u32[]{:S(2)}, u32[]{:S(2)}) collective-permute-start(bf16[8,64,768]{2,1,0:T(8,128)(2,1)S(1)} %get-tuple-element.4), channel_id=1, source_target_pairs={{8,0},{16,8},{24,16},{32,24},{40,32},{48,40},{56,48},{64,56},{72,6... | collective-permute-start | bytes 2359304 | tf_op jit(solution)/shard_map/ppermute | solution.py:19
  35.2 10.0 %copy-start.2 = (bf16[8,128,768]{2,1,0:T(8,128)(2,1)S(1)}, bf16[8,128,768]{2,1,0:T(8,128)(2,1)}, u32[]{:S(2)}) copy-start(bf16[8,128,768]{2,1,0:T(8,128)(2,1)} %param.5) | copy-start | bytes 4718596
  35.2 9.9 %copy-start.4 = (bf16[3,768,768]{2,1,0:T(8,128)(2,1)S(1)}, bf16[3,768,768]{2,1,0:T(8,128)(2,1)}, u32[]{:S(2)}) copy-start(bf16[3,768,768]{2,1,0:T(8,128)(2,1)} %param.4) | copy-start | bytes 10616836
  35.2 15.9 %collective-permute-start.3 = (bf16[8,64,768]{2,1,0:T(8,128)(2,1)S(1)}, bf16[8,64,768]{2,1,0:T(8,128)(2,1)S(1)}, u32[]{:S(2)}, u32[]{:S(2)}) collective-permute-start(bf16[8,64,768]{2,1,0:T(8,128)(2,1)S(1)} %get-tuple-element.3), channel_id=1, source_target_pairs={{0,8},{8,16},{16,24},{24,32},{32,40},{40,48},{48,56},{56,64},{64,7... | collective-permute-start | bytes 2359304 | tf_op jit(solution)/shard_map/ppermute | solution.py:17
  45.1 1.4 copy-start.6
Sparse Core Ops, SparseCore 0:
  31.8 154.5 reduce-scatter.4
  191.4 84.3 reduce-scatter.6
where the time goes:
time: 286 us; the launch traced here: 284 us
  waiting for transfers between devices  215 us (75%)
  matrix products  26.4 us (9%)
  between operations  14.2 us (5%)
  starting transfers between devices  13.9 us (5%)
  local copies, waits for them, and re-layouts  8.36 us (3%)
  other arithmetic  6.64 us (2%)
    reduce_scatter x1, waiting for transfers between devices, on_device(): lax.psum_scatter(partial_terms, 'seq', scatter_dimension=1, tiled=True)  131 us
    unnamed x3, waiting for transfers between devices  78.5 us
    dot_general x2, matrix products, on_device(): jnp.einsum('stc,cd->std', act_taps[kernel_tap_index], kernel[kernel_tap_i...  11.2 us
    ppermute x2, starting transfers between devices, padded(): lax.ppermute(head, axis, [((i + 1) % count, i) for i in range(ends)])  7.07 us
    ppermute x2, starting transfers between devices, padded(): lax.ppermute(tail, axis, [(i, (i + 1) % count) for i in range(ends)])  6.76 us
    unnamed x18, local copies, waits for them, and re-layouts  6.75 us
    dot_general x2, matrix products, on_device(): jnp.einsum('std,cd->stc', up_taps[kernel_tap_index], kernel[kernel_tap_in...  5.82 us
  transfers between devices with their start and end apart: 6, of which 4 were waited for; matrix products, arithmetic and copies ran while one was open for 9% of the time, Pallas kernels for 0%

commit v1 on v0

v1 whole, which is shorter than its diff:
```python
import functools
import math

import jax
import jax.numpy as jnp
from jax import lax
from jax.experimental import pallas as pl
from jax.experimental.pallas import tpu as pltpu
from jax.sharding import PartitionSpec as P

MESH = pl.DeviceIdType.MESH
BF16 = jnp.bfloat16
F32 = jnp.float32
SEQS = 8
HALF = 64
WIDTH = 768
ROWS = SEQS * HALF
TILE = 256
TILES = WIDTH // TILE
ROOT = math.sqrt(2.0 / math.pi)
CUBIC = 0.044715
FACTOR = 1.0 / math.sqrt(64 * 4096)
FULL_TILE = (0, 2, 3, 5)
SHARED_TILE = (1, 1, 4, 4)


def dot(a, b):
    return lax.dot_general(a, b, (((1,), (0,)), ((), ())), preferred_element_type=F32)


def dot_t(a, b):
    return lax.dot_general(a, b, (((1,), (1,)), ((), ())), preferred_element_type=F32)


def kernel(
    f_hbm, k_hbm, c_hbm, out_hbm, gin_hbm, wg_ref,
    f_v, c_v, k_v, a_v, at_v, d_v, c_halo, a_halo, conv, back, o_v, g_v,
    part, mate_part, ys, yr, xs, xr, zs, zr,
    in_sem, out_sem, halo_s, halo_r, core_s, core_r, y_s, y_r, x_s, x_r, z_s, z_r,
):
    s = lax.axis_index("seq")
    d = lax.axis_index("dp")
    core = lax.rem(s, 2)
    x = lax.rem(s // 2, 4)
    z_lo = s // 8
    y = d // 2
    z_hi = lax.rem(d, 2)
    z = z_hi * 4 + z_lo
    left = lax.rem(s + 31, 32)
    right = lax.rem(s + 1, 32)
    mate = s + 1 - 2 * core

    def y_partner(k):
        return {"seq": s, "dp": lax.rem(y + k, 4) * 2 + z_hi}

    def x_partner(k):
        return {"seq": (z_lo * 4 + lax.rem(x + k, 4)) * 2 + core, "dp": d}

    def z_partner(k):
        other = lax.rem(z + k, 8)
        return {"seq": (lax.rem(other, 4) * 4 + x) * 2 + core, "dp": y * 2 + other // 4}

    loads = []
    for half in range(2):
        rows = pl.ds(half * HALF, HALF)
        loads.append(pltpu.make_async_copy(f_hbm.at[:, rows, :], f_v.at[half], in_sem.at[half]))
    for half in range(2):
        rows = pl.ds(half * HALF, HALF)
        loads.append(pltpu.make_async_copy(c_hbm.at[:, rows, :], c_v.at[half], in_sem.at[2 + half]))
    loads.append(pltpu.make_async_copy(k_hbm, k_v, in_sem.at[4]))
    for load in loads:
        load.start()

    barrier = pltpu.get_barrier_semaphore()
    partners = [{"seq": left, "dp": d}, {"seq": right, "dp": d}]
    partners += [y_partner(k) for k in range(1, 4)]
    partners += [x_partner(k) for k in range(1, 4)]
    partners += [z_partner(k) for k in range(1, 8)]
    for partner in partners:
        pl.semaphore_signal(barrier, inc=1, device_id=partner, device_id_type=MESH)
    pl.semaphore_wait(barrier, len(partners))

    def remote(src, dst, send_sem, recv_sem, device):
        return pltpu.make_async_remote_copy(
            src_ref=src, dst_ref=dst, send_sem=send_sem, recv_sem=recv_sem,
            device_id=device, device_id_type=MESH,
        )

    def halo(i, src, dst):
        to_right = remote(src(1), dst.at[0], halo_s.at[2 * i], halo_r.at[2 * i], {"seq": right, "dp": d})
        to_left = remote(src(0), dst.at[1], halo_s.at[2 * i + 1], halo_r.at[2 * i + 1], {"seq": left, "dp": d})
        return to_right, to_left

    cot_halo = halo(0, lambda half: c_hbm.at[:, pl.ds(half * HALF, HALF), :], c_halo)
    act_halo = halo(1, lambda half: a_v.at[half], a_halo)

    def start_halo(copies):
        @pl.when(s < 31)
        def _():
            copies[0].start()

        @pl.when(s > 0)
        def _():
            copies[1].start()

    def receive_halo(copies, dst):
        @pl.when(s > 0)
        def _():
            copies[0].wait_recv()

        @pl.when(s == 0)
        def _():
            dst[0] = jnp.zeros(dst.shape[1:], BF16)

        @pl.when(s < 31)
        def _():
            copies[1].wait_recv()

        @pl.when(s == 31)
        def _():
            dst[1] = jnp.zeros(dst.shape[1:], BF16)

    def sent_halo(copies):
        @pl.when(s < 31)
        def _():
            copies[0].wait_send()

        @pl.when(s > 0)
        def _():
            copies[1].wait_send()

    start_halo(cot_halo)

    loads[0].wait()
    loads[1].wait()

    def activate(i, carry):
        half = i // 24
        pair = lax.rem(i // 6, 4)
        lanes = pl.ds(pl.multiple_of(lax.rem(i, 6) * 128, 128), 128)
        v = f_v[half, pl.ds(pair * 2, 2), :, lanes].reshape(128, 128).astype(F32)
        sq = v * v
        t = jnp.tanh(ROOT * v * (1.0 + CUBIC * sq))
        cdf = 0.5 * (1.0 + t)
        act = v * cdf
        slope = cdf + 0.5 * v * (1.0 - t * t) * (ROOT * (1.0 + 3.0 * CUBIC * sq))
        a_v[half, pl.ds(pair * 2, 2), :, lanes] = act.astype(BF16).reshape(2, HALF, 128)
        rows = pl.ds(pl.multiple_of(pair * 128, 128), 128)
        d_v[half, rows, lanes] = slope
        at_v[half, lanes, rows] = act.T.astype(BF16)
        return carry

    lax.fori_loop(0, 48, activate, 0)

    def cols_of(j):
        return pl.ds(pl.multiple_of(j * TILE, TILE), TILE)

    def cots(ref, half, cols):
        return ref[half, :, :, cols].reshape(ROWS, TILE)

    def rows_of(ref, half):
        return ref[half].reshape(ROWS, WIDTH)

    def grad_terms(tap, terms, add):
        def body(j, carry):
            cols = cols_of(j)
            total = dot(at_v[terms[0][0]], cots(terms[0][1], terms[0][2], cols))
            for act_half, ref, half in terms[1:]:
                total = total + dot(at_v[act_half], cots(ref, half, cols))
            total = total.reshape(4, 4, 2, 24, TILE)
            if add:
                total = total + part[tap, :, :, :, :, cols]
            part[tap, :, :, :, :, cols] = total
            return carry

        lax.fori_loop(0, TILES, body, 0)

    core_copy = [
        remote(part.at[tap, :, :, 1 - core], mate_part.at[tap], core_s.at[tap], core_r.at[tap], {"seq": mate, "dp": d})
        for tap in range(3)
    ]
    y_copy = [
        [
            remote(ys.at[lax.rem(y + k, 4), tap], yr.at[k - 1, tap], y_s.at[tap, k - 1], y_r.at[tap, k - 1], y_partner(k))
            for k in range(1, 4)
        ]
        for tap in range(3)
    ]
    x_copy = [
        [
            remote(xs.at[lax.rem(x + k, 4), tap], xr.at[k - 1, tap], x_s.at[tap, k - 1], x_r.at[tap, k - 1], x_partner(k))
            for k in range(1, 4)
        ]
        for tap in range(3)
    ]
    z_copy = [
        [
            remote(zs.at[lax.rem(z + k, 8), tap], zr.at[k - 1, tap], z_s.at[tap, k - 1], z_r.at[tap, k - 1], z_partner(k))
            for k in range(1, 8)
        ]
        for tap in range(3)
    ]

    lane = lax.broadcasted_iota(jnp.int32, (48, 128), 1)
    lane96 = lax.broadcasted_iota(jnp.int32, (96, 128), 1)

    def send_y(tap):
        core_copy[tap].wait_recv()

        def body(i, carry):
            total = part[tap, :, i, core] + mate_part[tap, :, i]
            total = total.reshape(96, WIDTH)
            for to in range(4):
                full = total[:, FULL_TILE[to] * 128 : FULL_TILE[to] * 128 + 128]
                shared = total[:, SHARED_TILE[to] * 128 : SHARED_TILE[to] * 128 + 128]
                a, b = shared[:48], shared[48:]
                if to % 2 == 0:
                    packed = jnp.where(lane < 64, a, pltpu.roll(b, 64, 1))
                else:
                    packed = jnp.where(lane < 64, pltpu.roll(a, 64, 1), b)
                ys[to, tap, i, :96] = full.astype(BF16)
                ys[to, tap, i, 96:] = packed.astype(BF16)
            return carry

        lax.fori_loop(0, 4, body, 0)
        for copy in y_copy[tap]:
            copy.start()

    def send_x(tap):
        for copy in y_copy[tap]:
            copy.wait_recv()

        def body(i, carry):
            total = ys[y, tap, i].astype(F32)
            for k in range(3):
                total = total + yr[k, tap, i].astype(F32)
            xs[i, tap] = total.astype(BF16)
            return carry

        lax.fori_loop(0, 4, body, 0)
        for copy in x_copy[tap]:
            copy.start()

    def send_z(tap):
        for copy in x_copy[tap]:
            copy.wait_recv()
        total = xs[x, tap].astype(F32)
        for k in range(3):
            total = total + xr[k, tap].astype(F32)
        full, packed = total[:96], total[96:]
        rest = jnp.concatenate([packed, pltpu.roll(packed, 64, 1)], axis=0)
        odd = lax.rem(y, 2) == 1
        first = jnp.where(odd, jnp.where(lane96 < 64, rest, pltpu.roll(full, 64, 1)), full)
        second = jnp.where(odd, pltpu.roll(full, 96, 1), pltpu.roll(jnp.where(lane96 >= 96, full, rest), 32, 1))
        zs[0:4, tap] = first.reshape(4, 24, 128)
        zs[4:8, tap] = second.reshape(4, 24, 128)
        for copy in z_copy[tap]:
            copy.start()

    def conv_inner(j, carry):
        cols = cols_of(j)
        head, tail = rows_of(a_v, 0), rows_of(a_v, 1)
        conv[0, :, cols] = dot(head, k_v[1, :, cols]) + dot(tail, k_v[2, :, cols])
        conv[1, :, cols] = dot(head, k_v[0, :, cols]) + dot(tail, k_v[1, :, cols])
        return carry

    def back_inner(j, carry):
        cols = cols_of(j)
        head, tail = rows_of(c_v, 0), rows_of(c_v, 1)
        back[0, :, cols] = dot_t(tail, k_v[0, cols, :]) + dot_t(head, k_v[1, cols, :])
        back[1, :, cols] = dot_t(tail, k_v[1, cols, :]) + dot_t(head, k_v[2, cols, :])
        return carry

    def back_outer(j, carry):
        cols = cols_of(j)
        for half, tap in ((0, 2), (1, 0)):
            total = back[half, :, cols] + dot_t(rows_of(c_halo, half), k_v[tap, cols, :])
            own = c_v[half, :, :, cols].reshape(ROWS, TILE).astype(F32)
            result = own + d_v[half, :, cols] * total
            g_v[half, :, :, cols] = result.astype(BF16).reshape(SEQS, HALF, TILE)
        return carry

    def conv_outer(j, carry):
        cols = cols_of(j)
        for half, tap in ((0, 0), (1, 2)):
            total = conv[half, :, cols] + dot(rows_of(a_halo, half), k_v[tap, :, cols])
            own = f_v[half, :, :, cols].reshape(ROWS, TILE).astype(F32)
            o_v[half, :, :, cols] = (own + total).astype(BF16).reshape(SEQS, HALF, TILE)
        return carry

    loads[2].wait()
    loads[3].wait()
    grad_terms(1, [(0, c_v, 0), (1, c_v, 1)], False)
    core_copy[1].start()
    grad_terms(0, [(0, c_v, 1)], False)
    grad_terms(2, [(1, c_v, 0)], False)
    send_y(1)
    loads[4].wait()
    lax.fori_loop(0, TILES, back_inner, 0)
    receive_halo(cot_halo, c_halo)
    start_halo(act_halo)
    grad_terms(0, [(1, c_halo, 1)], True)
    core_copy[0].start()
    grad_terms(2, [(0, c_halo, 0)], True)
    core_copy[2].start()
    send_x(1)
    send_y(0)
    send_y(2)
    lax.fori_loop(0, TILES, conv_inner, 0)
    lax.fori_loop(0, TILES, back_outer, 0)
    stores = []
    for half in range(2):
        rows = pl.ds(half * HALF, HALF)
        stores.append(pltpu.make_async_copy(g_v.at[half], gin_hbm.at[:, rows, :], out_sem.at[half]))
    stores[0].start()
    stores[1].start()
    send_z(1)
    send_x(0)
    receive_halo(act_halo, a_halo)
    lax.fori_loop(0, TILES, conv_outer, 0)
    for half in range(2):
        rows = pl.ds(half * HALF, HALF)
        stores.append(pltpu.make_async_copy(o_v.at[half], out_hbm.at[:, rows, :], out_sem.at[2 + half]))
    stores[2].start()
    stores[3].start()
    send_z(0)
    send_x(2)
    send_z(2)
    for tap in (1, 0, 2):
        for copy in z_copy[tap]:
            copy.wait_recv()
        total = zs[z, tap]
        for k in range(7):
            total = total + zr[k, tap]
        wg_ref[tap] = (total * FACTOR)[:, :96]

    sent_halo(cot_halo)
    sent_halo(act_halo)
    for tap in range(3):
        core_copy[tap].wait_send()
        for copy in y_copy[tap] + x_copy[tap] + z_copy[tap]:
            copy.wait_send()
    for store in stores:
        store.wait()


def on_device(features, weights, cotangent):
    block = jax.ShapeDtypeStruct(features.shape, BF16)
    hbm = pl.BlockSpec(memory_space=pl.ANY)
    vmem = pltpu.VMEM
    dma = pltpu.SemaphoreType.DMA
    halves = (2, SEQS, HALF, WIDTH)
    return pl.pallas_call(
        kernel,
        out_shape=(block, block, jax.ShapeDtypeStruct((3, 24, 96), F32)),
        in_specs=[hbm, hbm, hbm],
        out_specs=(hbm, hbm, pl.BlockSpec(memory_space=pltpu.VMEM)),
        scratch_shapes=[
            vmem(halves, BF16),
            vmem(halves, BF16),
            vmem((3, WIDTH, WIDTH), BF16),
            vmem(halves, BF16),
            vmem((2, WIDTH, ROWS), BF16),
            vmem((2, ROWS, WIDTH), F32),
            vmem(halves, BF16),
            vmem(halves, BF16),
            vmem((2, ROWS, WIDTH), F32),
            vmem((2, ROWS, WIDTH), F32),
            vmem(halves, BF16),
            vmem(halves, BF16),
            vmem((3, 4, 4, 2, 24, WIDTH), F32),
            vmem((3, 4, 4, 24, WIDTH), F32),
            vmem((4, 3, 4, 144, 128), BF16),
            vmem((3, 3, 4, 144, 128), BF16),
            vmem((4, 3, 144, 128), BF16),
            vmem((3, 3, 144, 128), BF16),
            vmem((8, 3, 24, 128), F32),
            vmem((7, 3, 24, 128), F32),
            dma((5,)), dma((4,)), dma((4,)), dma((4,)), dma((3,)), dma((3,)),
            dma((3, 3)), dma((3, 3)), dma((3, 3)), dma((3, 3)), dma((3, 7)), dma((3, 7)),
        ],
        compiler_params=pltpu.CompilerParams(
            collective_id=0, has_side_effects=True, vmem_limit_bytes=58 * 1024 * 1024
        ),
        cost_estimate=pl.CostEstimate(
            flops=18 * 2 * ROWS * WIDTH * WIDTH, bytes_accessed=10 * 1024 * 1024, transcendentals=2 * ROWS * WIDTH
        ),
    )(features, weights, cotangent)


def solution(mesh):
    in_specs = (P("dp", "seq", None), P(), P("dp", "seq", None))
    out_specs = (P("dp", "seq", None), P("dp", "seq", None), P(None, "seq", "dp"))
    return jax.shard_map(
        on_device, mesh=mesh, in_specs=in_specs, out_specs=out_specs, check_vma=False
    )
```

time: 286 us -> 60.2 us (0.21)
  waiting for transfers between devices: 215 us -> 0 us
  Pallas kernels: 0 us -> 54.5 us
  matrix products: 26.4 us -> 0 us
  starting transfers between devices: 13.9 us -> 0 us
  between operations: 14.2 us -> 0.65 us
  other arithmetic: 6.64 us -> 0 us
  local copies, waits for them, and re-layouts: 8.36 us -> 4.54 us
    reduce_scatter x1 -> x0, waiting for transfers between devices: 131 us -> none  [on_device(): lax.psum_scatter(partial_terms, 'seq', scatter_dimension=1, tiled=True)]
    unnamed x3 -> x0, waiting for transfers between devices: 78.5 us -> none
    pallas_call x0 -> x1, Pallas kernels: none -> 54.5 us  [on_device(): pl.pallas_call(kernel, out_shape=(block, block, jax.ShapeDtypeStruct((3,...]
    dot_general x9 -> x0, matrix products: 26.4 us -> none  [the longest x2 11.2 us: on_device(): jnp.einsum('stc,cd->std', act_taps[kernel_tap_index], kernel[kernel_tap_i...]
    ppermute x4 -> x0, starting transfers between devices: 13.8 us -> none  [the longest x2 7.07 us: padded(): lax.ppermute(head, axis, [((i + 1) % count, i) for i in range(ends)])]
    ppermute x4 -> x0, waiting for transfers between devices: 5.47 us -> none  [the longest x2 5.12 us: padded(): lax.ppermute(head, axis, [((i + 1) % count, i) for i in range(ends)])]
    another operation x1 -> x0, other arithmetic: 3.36 us -> none  [on_device(): jnp.stack([jnp.einsum('stc,std->cd', act_taps[kernel_tap_index], cotangen...]
    unnamed x18 -> x7, local copies, waits for them, and re-layouts: 6.75 us -> 4.54 us
  transfers between devices with their start and end apart: 6 -> 0, of which waited for: 4 -> 0; matrix products, arithmetic and copies ran while one was open for 9% -> 0% of each run, Pallas kernels for 0% -> 0%
where the time goes in v1:
time: 60.2 us; the launch traced here: 59.7 us
  Pallas kernels  54.5 us (91%)
  local copies, waits for them, and re-layouts  4.54 us (8%)
  between operations  0.65 us (1%)
    pallas_call x1, Pallas kernels, on_device(): pl.pallas_call(kernel, out_shape=(block, block, jax.ShapeDtypeStruct((3,...  54.5 us
    unnamed x7, local copies, waits for them, and re-layouts  4.54 us

profile of v1, /device:TPU:1, one launch (start us, length us, event | category | flops | bytes accessed | tf_op | source)
XLA Modules:
  0.0 59.7 jit_solution(7844494050270064379)
XLA Ops:
  0.6 54.5 %shard_map.58 = (bf16[8,128,768]{2,1,0:T(8,128)(2,1)}, bf16[8,128,768]{2,1,0:T(8,128)(2,1)}, f32[3,24,96]{2,1,0:T(8,128)}) custom-call(bf16[8,128,768]{2,1,0:T(8,128)(2,1)} %f_hbm.1, bf16[3,768,768]{2,1,0:T(8,128)(2,1)} %k_hbm.1, bf16[8,128,768]{2,1,0:T(8,128)(2,1)} %c_hbm.1), custom_call_target="tpu_custom_call" | custom-call | flops 10871635968 | bytes 10485760 | tf_op jit(solution)/shard_map/pallas_call | solution.py:353
  55.1 0.0 copy-start
  55.1 2.8 %copy.9 = bf16[8,128,768]{2,1,0:T(8,128)(2,1)} copy(bf16[8,128,768]{2,1,0:T(8,128)(2,1)} %get-tuple-element.6) | data formatting | bytes 3145728
  57.9 0.0 copy-done
  57.9 0.0 copy-start.1
  57.9 1.1 %copy.10 = bf16[8,128,768]{2,1,0:T(8,128)(2,1)} copy(bf16[8,128,768]{2,1,0:T(8,128)(2,1)S(1)} %copy-done) | data formatting | bytes 3145728
  59.1 0.0 copy-done.1
  59.1 0.6 %copy.11 = f32[3,24,96]{2,1,0:T(8,128)} copy(f32[3,24,96]{2,1,0:T(8,128)S(1)} %copy-done.1) | data formatting | bytes 55296
Async XLA Ops:
  55.1 2.8 %copy-start = (bf16[8,128,768]{2,1,0:T(8,128)(2,1)S(1)}, bf16[8,128,768]{2,1,0:T(8,128)(2,1)}, u32[]{:S(2)}) copy-start(bf16[8,128,768]{2,1,0:T(8,128)(2,1)} %get-tuple-element.7) | copy-start | bytes 4718596
  57.9 1.1 %copy-start.1 = (f32[3,24,96]{2,1,0:T(8,128)S(1)}, f32[3,24,96]{2,1,0:T(8,128)}, u32[]{:S(2)}) copy-start(f32[3,24,96]{2,1,0:T(8,128)} %get-tuple-element.8) | copy-start | bytes 82948

commit v2 on v1

--- a/solution.py
+++ b/solution.py
@@ -35,8 +35,9 @@
 def kernel(
     f_hbm, k_hbm, c_hbm, out_hbm, gin_hbm, wg_ref,
     f_v, c_v, k_v, a_v, at_v, d_v, c_halo, a_halo, conv, back, o_v, g_v,
-    part, mate_part, ys, yr, xs, xr, zs, zr,
+    part, mate_part, ys, yr, xs, xr, zs, zr, xs2, xr2, ys2, yr2,
     in_sem, out_sem, halo_s, halo_r, core_s, core_r, y_s, y_r, x_s, x_r, z_s, z_r,
+    y2_s, y2_r, x2_s, x2_r,
 ):
     s = lax.axis_index("seq")
     d = lax.axis_index("dp")
@@ -103,22 +104,20 @@
         def _():
             copies[1].start()
 
-    def receive_halo(copies, dst):
-        @pl.when(s > 0)
-        def _():
-            copies[0].wait_recv()
-
-        @pl.when(s == 0)
-        def _():
-            dst[0] = jnp.zeros(dst.shape[1:], BF16)
-
-        @pl.when(s < 31)
-        def _():
-            copies[1].wait_recv()
-
-        @pl.when(s == 31)
-        def _():
-            dst[1] = jnp.zeros(dst.shape[1:], BF16)
+    def receive_early(i, dst):
+        slot = 1 - core
+        remote(dst.at[0], dst.at[slot], halo_s.at[2 * i], halo_r.at[2 * i + slot], {"seq": mate, "dp": d}).wait_recv()
+
+    def receive_late(i, dst):
+        inside = jnp.logical_and(s > 0, s < 31)
+
+        @pl.when(inside)
+        def _():
+            remote(dst.at[0], dst.at[core], halo_s.at[2 * i], halo_r.at[2 * i + core], {"seq": mate, "dp": d}).wait_recv()
+
+        @pl.when(jnp.logical_not(inside))
+        def _():
+            dst[core] = jnp.zeros(dst.shape[1:], BF16)
 
     def sent_halo(copies):
         @pl.when(s < 31)
@@ -135,22 +134,29 @@
     loads[1].wait()
 
     def activate(i, carry):
+        half = i // 24
+        pair = lax.rem(i // 6, 4)
+        lanes = pl.ds(pl.multiple_of(lax.rem(i, 6) * 128, 128), 128)
+        v = f_v[half, pl.ds(pair * 2, 2), :, lanes].reshape(128, 128).astype(F32)
+        t = jnp.tanh(ROOT * v * (1.0 + CUBIC * (v * v)))
+        act = v * (0.5 * (1.0 + t))
+        a_v[half, pl.ds(pair * 2, 2), :, lanes] = act.astype(BF16).reshape(2, HALF, 128)
+        rows = pl.ds(pl.multiple_of(pair * 128, 128), 128)
+        at_v[half, lanes, rows] = act.T.astype(BF16)
+        return carry
+
+    lax.fori_loop(0, 48, activate, 0, unroll=2)
+
+    def derive(i, carry):
         half = i // 24
         pair = lax.rem(i // 6, 4)
         lanes = pl.ds(pl.multiple_of(lax.rem(i, 6) * 128, 128), 128)
         v = f_v[half, pl.ds(pair * 2, 2), :, lanes].reshape(128, 128).astype(F32)
         sq = v * v
         t = jnp.tanh(ROOT * v * (1.0 + CUBIC * sq))
-        cdf = 0.5 * (1.0 + t)
-        act = v * cdf
-        slope = cdf + 0.5 * v * (1.0 - t * t) * (ROOT * (1.0 + 3.0 * CUBIC * sq))
-        a_v[half, pl.ds(pair * 2, 2), :, lanes] = act.astype(BF16).reshape(2, HALF, 128)
-        rows = pl.ds(pl.multiple_of(pair * 128, 128), 128)
-        d_v[half, rows, lanes] = slope
-        at_v[half, lanes, rows] = act.T.astype(BF16)
-        return carry
-
-    lax.fori_loop(0, 48, activate, 0)
+        slope = 0.5 * (1.0 + t) + 0.5 * v * (1.0 - t * t) * (ROOT * (1.0 + 3.0 * CUBIC * sq))
+        d_v[half, pl.ds(pl.multiple_of(pair * 128, 128), 128), lanes] = slope
+        return carry
 
     def cols_of(j):
         return pl.ds(pl.multiple_of(j * TILE, TILE), TILE)
@@ -161,7 +167,13 @@
     def rows_of(ref, half):
         return ref[half].reshape(ROWS, WIDTH)
 
-    def grad_terms(tap, terms, add):
+    def core_copy(tap, j):
+        return remote(
+            part.at[tap, j, :, :, 1 - core], mate_part.at[tap, j], core_s.at[tap, j], core_r.at[tap, j],
+            {"seq": mate, "dp": d},
+        )
+
+    def grad_terms(tap, terms, add, send):
         def body(j, carry):
             cols = cols_of(j)
             total = dot(at_v[terms[0][0]], cots(terms[0][1], terms[0][2], cols))
@@ -169,65 +181,113 @@
                 total = total + dot(at_v[act_half], cots(ref, half, cols))
             total = total.reshape(4, 4, 2, 24, TILE)
             if add:
-                total = total + part[tap, :, :, :, :, cols]
-            part[tap, :, :, :, :, cols] = total
+                total = total + part[tap, j]
+            part[tap, j] = total
+            if send:
+                core_copy(tap, j).start()
             return carry
 
         lax.fori_loop(0, TILES, body, 0)
 
-    core_copy = [
-        remote(part.at[tap, :, :, 1 - core], mate_part.at[tap], core_s.at[tap], core_r.at[tap], {"seq": mate, "dp": d})
-        for tap in range(3)
-    ]
-    y_copy = [
-        [
-            remote(ys.at[lax.rem(y + k, 4), tap], yr.at[k - 1, tap], y_s.at[tap, k - 1], y_r.at[tap, k - 1], y_partner(k))
+    def y_copy(tap):
+        return [
+        remote(ys.at[lax.rem(y + k, 4), tap], yr.at[k - 1, tap], y_s.at[tap, k - 1], y_r.at[tap, k - 1], y_partner(k))
+        for k in range(1, 4)
+        ]
+
+    def x_copy(tap):
+        return [
+        remote(xs.at[lax.rem(x + k, 4), tap], xr.at[k - 1, tap], x_s.at[tap, k - 1], x_r.at[tap, k - 1], x_partner(k))
+        for k in range(1, 4)
+        ]
+
+    def z_copy(tap):
+        return [
+        remote(zs.at[lax.rem(z + k, 8), tap], zr.at[k - 1, tap], z_s.at[tap, k - 1], z_r.at[tap, k - 1], z_partner(k))
+        for k in range(1, 8)
+        ]
+
+
+    def x_first(tap):
+        return [
+            remote(xs2.at[lax.rem(x + k, 4), tap], xr2.at[k - 1, tap], x2_s.at[tap, k - 1], x2_r.at[tap, k - 1], x_partner(k))
             for k in range(1, 4)
         ]
-        for tap in range(3)
-    ]
-    x_copy = [
-        [
-            remote(xs.at[lax.rem(x + k, 4), tap], xr.at[k - 1, tap], x_s.at[tap, k - 1], x_r.at[tap, k - 1], x_partner(k))
-            for k in range(1, 4)
+
+    def y_second(tap):
+        return [
+        remote(ys2.at[lax.rem(y + k, 4), tap], yr2.at[k - 1, tap], y2_s.at[tap, k - 1], y2_r.at[tap, k - 1], y_partner(k))
+        for k in range(1, 4)
         ]
-        for tap in range(3)
-    ]
-    z_copy = [
-        [
-            remote(zs.at[lax.rem(z + k, 8), tap], zr.at[k - 1, tap], z_s.at[tap, k - 1], z_r.at[tap, k - 1], z_partner(k))
-            for k in range(1, 8)
-        ]
-        for tap in range(3)
-    ]
-
-    lane = lax.broadcasted_iota(jnp.int32, (48, 128), 1)
+
+    lane16 = lax.broadcasted_iota(jnp.int32, (16, 128), 1)
+    lane32 = lax.broadcasted_iota(jnp.int32, (32, 128), 1)
     lane96 = lax.broadcasted_iota(jnp.int32, (96, 128), 1)
 
+    def columns_for(to, tiles, lane):
+        full = tiles[FULL_TILE[to]]
+        shared = tiles[SHARED_TILE[to]]
+        a, b = shared[: lane.shape[0]], shared[lane.shape[0] :]
+        if to % 2 == 0:
+            return full, jnp.where(lane < 64, a, pltpu.roll(b, 64, 1))
+        return full, jnp.where(lane < 64, pltpu.roll(a, 64, 1), b)
+
+    def receive_core(tap):
+        for j in range(TILES):
+            core_copy(tap, j).wait_recv()
+
     def send_y(tap):
-        core_copy[tap].wait_recv()
-
         def body(i, carry):
-            total = part[tap, :, i, core] + mate_part[tap, :, i]
-            total = total.reshape(96, WIDTH)
+            tiles = []
+            for j in range(TILES):
+                total = part[tap, j, :, i, core, :16] + mate_part[tap, j, :, i, :16]
+                total = total.reshape(64, TILE)
+                tiles += [total[:, :128], total[:, 128:]]
             for to in range(4):
-                full = total[:, FULL_TILE[to] * 128 : FULL_TILE[to] * 128 + 128]
-                shared = total[:, SHARED_TILE[to] * 128 : SHARED_TILE[to] * 128 + 128]
-                a, b = shared[:48], shared[48:]
-                if to % 2 == 0:
-                    packed = jnp.where(lane < 64, a, pltpu.roll(b, 64, 1))
-                else:
-                    packed = jnp.where(lane < 64, pltpu.roll(a, 64, 1), b)
-                ys[to, tap, i, :96] = full.astype(BF16)
-                ys[to, tap, i, 96:] = packed.astype(BF16)
+                full, packed = columns_for(to, tiles, lane32)
+                ys[to, tap, i, :64] = full.astype(BF16)
+                ys[to, tap, i, 64:] = packed.astype(BF16)
             return carry
 
         lax.fori_loop(0, 4, body, 0)
-        for copy in y_copy[tap]:
+        for copy in y_copy(tap):
             copy.start()
 
+    def send_x_first(tap):
+        def body(i, carry):
+            for j in range(TILES):
+                total = part[tap, j, :, i, core, 16:] + mate_part[tap, j, :, i, 16:]
+                xs2[i, tap, :, j * TILE : (j + 1) * TILE] = total.reshape(32, TILE).astype(BF16)
+            return carry
+
+        lax.fori_loop(0, 4, body, 0)
+        for copy in x_first(tap):
+            copy.start()
+
+    def send_y_second(tap):
+        for copy in x_first(tap):
+            copy.wait_recv()
+        tiles = []
+        for j in range(6):
+            cols = slice(j * 128, j * 128 + 128)
+            total = xs2[x, tap, :, cols].astype(F32)
+            for k in range(3):
+                total = total + xr2[k, tap, :, cols].astype(F32)
+            tiles.append(total)
+        for to in range(4):
+            full, packed = columns_for(to, tiles, lane16)
+            ys2[to, tap, :32] = full.astype(BF16)
+            ys2[to, tap, 32:] = packed.astype(BF16)
+        for copy in y_second(tap):
+            copy.start()
+
+    def send_first(tap):
+        receive_core(tap)
+        send_y(tap)
+        send_x_first(tap)
+
     def send_x(tap):
-        for copy in y_copy[tap]:
+        for copy in y_copy(tap):
             copy.wait_recv()
 
         def body(i, carry):
@@ -238,23 +298,31 @@
             return carry
 
         lax.fori_loop(0, 4, body, 0)
-        for copy in x_copy[tap]:
+        for copy in x_copy(tap):
             copy.start()
 
     def send_z(tap):
-        for copy in x_copy[tap]:
+        for copy in x_copy(tap) + y_second(tap):
             copy.wait_recv()
-        total = xs[x, tap].astype(F32)
-        for k in range(3):
-            total = total + xr[k, tap].astype(F32)
-        full, packed = total[:96], total[96:]
-        rest = jnp.concatenate([packed, pltpu.roll(packed, 64, 1)], axis=0)
+
+        def gathered(own, others, rows):
+            total = own.astype(F32)
+            for k in range(3):
+                total = total + others[k, tap].astype(F32)
+            packed = total[4 * rows :]
+            rest = jnp.concatenate([packed, pltpu.roll(packed, 64, 1)], axis=0)
+            return total[: 4 * rows].reshape(4, rows, 128), rest.reshape(4, rows, 128)
+
+        full_a, rest_a = gathered(xs[x, tap], xr, 16)
+        full_b, rest_b = gathered(ys2[y, tap], yr2, 8)
+        full = jnp.concatenate([full_a, full_b], axis=1).reshape(96, 128)
+        rest = jnp.concatenate([rest_a, rest_b], axis=1).reshape(96, 128)
         odd = lax.rem(y, 2) == 1
         first = jnp.where(odd, jnp.where(lane96 < 64, rest, pltpu.roll(full, 64, 1)), full)
         second = jnp.where(odd, pltpu.roll(full, 96, 1), pltpu.roll(jnp.where(lane96 >= 96, full, rest), 32, 1))
         zs[0:4, tap] = first.reshape(4, 24, 128)
         zs[4:8, tap] = second.reshape(4, 24, 128)
-        for copy in z_copy[tap]:
+        for copy in z_copy(tap):
             copy.start()
 
     def conv_inner(j, carry):
@@ -288,46 +356,55 @@
             o_v[half, :, :, cols] = (own + total).astype(BF16).reshape(SEQS, HALF, TILE)
         return carry
 
+    stores = []
+
+    def store(i, source, target):
+        for half in range(2):
+            rows = pl.ds(half * HALF, HALF)
+            stores.append(pltpu.make_async_copy(source.at[half], target.at[:, rows, :], out_sem.at[2 * i + half]))
+            stores[-1].start()
+
+    early, late = 2 * core, 2 - 2 * core
+
+    def grad_outer(tap, half):
+        grad_terms(tap, [(half, c_halo, half)], True, True)
+
     loads[2].wait()
     loads[3].wait()
-    grad_terms(1, [(0, c_v, 0), (1, c_v, 1)], False)
-    core_copy[1].start()
-    grad_terms(0, [(0, c_v, 1)], False)
-    grad_terms(2, [(1, c_v, 0)], False)
-    send_y(1)
+    grad_terms(1, [(0, c_v, 0), (1, c_v, 1)], False, True)
+    grad_terms(0, [(0, c_v, 1)], False, False)
+    send_first(1)
+    grad_terms(2, [(1, c_v, 0)], False, False)
+    receive_early(0, c_halo)
+    grad_outer(early, 1 - core)
     loads[4].wait()
-    lax.fori_loop(0, TILES, back_inner, 0)
-    receive_halo(cot_halo, c_halo)
+    lax.fori_loop(0, 1, back_inner, 0)
+    receive_late(0, c_halo)
+    grad_outer(late, core)
+    send_first(late)
+    send_first(early)
     start_halo(act_halo)
-    grad_terms(0, [(1, c_halo, 1)], True)
-    core_copy[0].start()
-    grad_terms(2, [(0, c_halo, 0)], True)
-    core_copy[2].start()
     send_x(1)
-    send_y(0)
-    send_y(2)
-    lax.fori_loop(0, TILES, conv_inner, 0)
+    send_y_second(1)
+    lax.fori_loop(1, TILES, back_inner, 0)
+    lax.fori_loop(0, 48, derive, 0, unroll=2)
+    send_z(1)
+    send_x(late)
+    send_y_second(late)
     lax.fori_loop(0, TILES, back_outer, 0)
-    stores = []
-    for half in range(2):
-        rows = pl.ds(half * HALF, HALF)
-        stores.append(pltpu.make_async_copy(g_v.at[half], gin_hbm.at[:, rows, :], out_sem.at[half]))
-    stores[0].start()
-    stores[1].start()
-    send_z(1)
-    send_x(0)
-    receive_halo(act_halo, a_halo)
+    store(0, g_v, gin_hbm)
+    send_x(early)
+    send_y_second(early)
+    lax.fori_loop(0, 2, conv_inner, 0)
+    send_z(late)
+    send_z(early)
+    lax.fori_loop(2, TILES, conv_inner, 0)
+    receive_early(1, a_halo)
+    receive_late(1, a_halo)
     lax.fori_loop(0, TILES, conv_outer, 0)
-    for half in range(2):
-        rows = pl.ds(half * HALF, HALF)
-        stores.append(pltpu.make_async_copy(o_v.at[half], out_hbm.at[:, rows, :], out_sem.at[2 + half]))
-    stores[2].start()
-    stores[3].start()
-    send_z(0)
-    send_x(2)
-    send_z(2)
-    for tap in (1, 0, 2):
-        for copy in z_copy[tap]:
+    store(1, o_v, out_hbm)
+    for tap in (1, late, early):
+        for copy in z_copy(tap):
             copy.wait_recv()
         total = zs[z, tap]
         for k in range(7):
@@ -337,11 +414,12 @@
     sent_halo(cot_halo)
     sent_halo(act_halo)
     for tap in range(3):
-        core_copy[tap].wait_send()
-        for copy in y_copy[tap] + x_copy[tap] + z_copy[tap]:
+        for j in range(TILES):
+            core_copy(tap, j).wait_send()
+        for copy in y_copy(tap) + x_copy(tap) + z_copy(tap) + x_first(tap) + y_second(tap):
             copy.wait_send()
-    for store in stores:
-        store.wait()
+    for pending in stores:
+        pending.wait()
 
 
 def on_device(features, weights, cotangent):
@@ -368,19 +446,24 @@
             vmem((2, ROWS, WIDTH), F32),
             vmem(halves, BF16),
             vmem(halves, BF16),
-            vmem((3, 4, 4, 2, 24, WIDTH), F32),
-            vmem((3, 4, 4, 24, WIDTH), F32),
-            vmem((4, 3, 4, 144, 128), BF16),
-            vmem((3, 3, 4, 144, 128), BF16),
-            vmem((4, 3, 144, 128), BF16),
-            vmem((3, 3, 144, 128), BF16),
+            vmem((3, TILES, 4, 4, 2, 24, TILE), F32),
+            vmem((3, TILES, 4, 4, 24, TILE), F32),
+            vmem((4, 3, 4, 96, 128), BF16),
+            vmem((3, 3, 4, 96, 128), BF16),
+            vmem((4, 3, 96, 128), BF16),
+            vmem((3, 3, 96, 128), BF16),
             vmem((8, 3, 24, 128), F32),
             vmem((7, 3, 24, 128), F32),
-            dma((5,)), dma((4,)), dma((4,)), dma((4,)), dma((3,)), dma((3,)),
+            vmem((4, 3, 32, WIDTH), BF16),
+            vmem((3, 3, 32, WIDTH), BF16),
+            vmem((4, 3, 48, 128), BF16),
+            vmem((3, 3, 48, 128), BF16),
+            dma((5,)), dma((4,)), dma((4,)), dma((4,)), dma((3, 3)), dma((3, 3)),
             dma((3, 3)), dma((3, 3)), dma((3, 3)), dma((3, 3)), dma((3, 7)), dma((3, 7)),
+            dma((3, 3)), dma((3, 3)), dma((3, 3)), dma((3, 3)),
         ],
         compiler_params=pltpu.CompilerParams(
-            collective_id=0, has_side_effects=True, vmem_limit_bytes=58 * 1024 * 1024
+            collective_id=0, has_side_effects=True, vmem_limit_bytes=50 * 1024 * 1024
         ),
         cost_estimate=pl.CostEstimate(
             flops=18 * 2 * ROWS * WIDTH * WIDTH, bytes_accessed=10 * 1024 * 1024, transcendentals=2 * ROWS * WIDTH

time: 60.2 us -> 55.3 us (0.919)
  Pallas kernels: 54.5 us -> 51.7 us
  local copies, waits for them, and re-layouts: 4.54 us -> 2.9 us
    pallas_call x1, Pallas kernels: 54.5 us -> 51.7 us  [on_device(): pl.pallas_call(kernel, out_shape=(block, block, jax.ShapeDtypeStruct((3,...]
    unnamed x7 -> x3, local copies, waits for them, and re-layouts: 4.54 us -> 2.9 us
where the time goes in v2:
time: 55.3 us; the launch traced here: 55.2 us
  Pallas kernels  51.7 us (93%)
  local copies, waits for them, and re-layouts  2.9 us (5%)
  between operations  0.64 us (1%)
    pallas_call x1, Pallas kernels, on_device(): pl.pallas_call(kernel, out_shape=(block, block, jax.ShapeDtypeStruct((3,...  51.7 us
    unnamed x3, local copies, waits for them, and re-layouts  2.9 us

profile of v2, /device:TPU:1, one launch (start us, length us, event | category | flops | bytes accessed | tf_op | source)
XLA Modules:
  0.0 55.2 jit_solution(7601280296827215809)
XLA Ops:
  0.6 51.7 %shard_map.58 = (bf16[8,128,768]{2,1,0:T(8,128)(2,1)S(1)}, bf16[8,128,768]{2,1,0:T(8,128)(2,1)S(1)}, f32[3,24,96]{2,1,0:T(8,128)S(1)}) custom-call(bf16[8,128,768]{2,1,0:T(8,128)(2,1)} %f_hbm.1, bf16[3,768,768]{2,1,0:T(8,128)(2,1)} %k_hbm.1, bf16[8,128,768]{2,1,0:T(8,128)(2,1)} %c_hbm.1), custom_call_target="tpu_custom_call" | custom-call | flops 10871635968 | bytes 10485760 | tf_op jit(solution)/shard_map/pallas_call | solution.py:431
  52.3 1.1 %copy.9 = bf16[8,128,768]{2,1,0:T(8,128)(2,1)} copy(bf16[8,128,768]{2,1,0:T(8,128)(2,1)S(1)} %get-tuple-element.6) | data formatting | bytes 3145728
  53.5 1.1 %copy.10 = bf16[8,128,768]{2,1,0:T(8,128)(2,1)} copy(bf16[8,128,768]{2,1,0:T(8,128)(2,1)S(1)} %get-tuple-element.7) | data formatting | bytes 3145728
  54.6 0.6 %copy.11 = f32[3,24,96]{2,1,0:T(8,128)} copy(f32[3,24,96]{2,1,0:T(8,128)S(1)} %get-tuple-element.8) | data formatting | bytes 55296

commit v3 on v2

--- a/solution.py
+++ b/solution.py
@@ -20,8 +20,10 @@
 ROOT = math.sqrt(2.0 / math.pi)
 CUBIC = 0.044715
 FACTOR = 1.0 / math.sqrt(64 * 4096)
-FULL_TILE = (0, 2, 3, 5)
-SHARED_TILE = (1, 1, 4, 4)
+PAIRS = ((0, 2), (3, 5), (1, 4))
+CHUNKS = ((0, 1), (2,))
+SLICES = (((0, 128), (256, 256), (640, 128)), ((128, 128), (512, 128)))
+PIECES = ((0, 5), (5, 3))
 
 
 def dot(a, b):
@@ -87,37 +89,53 @@
             device_id=device, device_id_type=MESH,
         )
 
-    def halo(i, src, dst):
-        to_right = remote(src(1), dst.at[0], halo_s.at[2 * i], halo_r.at[2 * i], {"seq": right, "dp": d})
-        to_left = remote(src(0), dst.at[1], halo_s.at[2 * i + 1], halo_r.at[2 * i + 1], {"seq": left, "dp": d})
+    def halo(i, src, dst, where):
+        to_right = remote(src(1), dst.at[(0, *where)], halo_s.at[2 * i], halo_r.at[2 * i], {"seq": right, "dp": d})
+        to_left = remote(src(0), dst.at[(1, *where)], halo_s.at[2 * i + 1], halo_r.at[2 * i + 1], {"seq": left, "dp": d})
         return to_right, to_left
 
-    cot_halo = halo(0, lambda half: c_hbm.at[:, pl.ds(half * HALF, HALF), :], c_halo)
-    act_halo = halo(1, lambda half: a_v.at[half], a_halo)
-
-    def start_halo(copies):
+    every = slice(None)
+    cot_parts, act_parts = [], []
+    for chunk in SLICES:
+        cot_parts.append([(len(cot_parts) * 3 + i, (every, every, pl.ds(*cols))) for i, cols in enumerate(chunk)])
+    for i, piece in enumerate(PIECES):
+        act_parts.append([(5 + i, (pl.ds(*piece),))])
+    cot_halo = [[halo(i, lambda half, p=p: c_v.at[(half, *p)], c_halo, p) for i, p in chunk] for chunk in cot_parts]
+    act_halo = [[halo(i, lambda half, p=p: a_v.at[(half, *p)], a_halo, p) for i, p in chunk] for chunk in act_parts]
+
+    def start_halo(chunk):
         @pl.when(s < 31)
         def _():
-            copies[0].start()
+            for copies in chunk:
+                copies[0].start()
 
         @pl.when(s > 0)
         def _():
-            copies[1].start()
-
-    def receive_early(i, dst):
-        slot = 1 - core
-        remote(dst.at[0], dst.at[slot], halo_s.at[2 * i], halo_r.at[2 * i + slot], {"seq": mate, "dp": d}).wait_recv()
-
-    def receive_late(i, dst):
+            for copies in chunk:
+                copies[1].start()
+
+    def halo_into(i, dst, slot, where):
+        return remote(
+            dst.at[(0, *where)], dst.at[(slot, *where)], halo_s.at[2 * i], halo_r.at[2 * i + slot], {"seq": mate, "dp": d}
+        )
+
+    def receive_early(dst, parts):
+        for i, where in parts:
+            halo_into(i, dst, 1 - core, where).wait_recv()
+
+    def receive_late(dst, parts):
         inside = jnp.logical_and(s > 0, s < 31)
 
         @pl.when(inside)
         def _():
-            remote(dst.at[0], dst.at[core], halo_s.at[2 * i], halo_r.at[2 * i + core], {"seq": mate, "dp": d}).wait_recv()
+            for i, where in parts:
+                halo_into(i, dst, core, where).wait_recv()
 
         @pl.when(jnp.logical_not(inside))
         def _():
-            dst[core] = jnp.zeros(dst.shape[1:], BF16)
+            for _, where in parts:
+                blank = dst.at[(core, *where)]
+                blank[...] = jnp.zeros(blank.shape, BF16)
 
     def sent_halo(copies):
         @pl.when(s < 31)
@@ -128,7 +146,10 @@
         def _():
             copies[1].wait_send()
 
-    start_halo(cot_halo)
+    loads[2].wait()
+    loads[3].wait()
+    for chunk in cot_halo:
+        start_halo(chunk)
 
     loads[0].wait()
     loads[1].wait()
@@ -161,8 +182,9 @@
     def cols_of(j):
         return pl.ds(pl.multiple_of(j * TILE, TILE), TILE)
 
-    def cots(ref, half, cols):
-        return ref[half, :, :, cols].reshape(ROWS, TILE)
+    def cots(ref, half, j):
+        tiles = [ref[half, :, :, t * 128 : t * 128 + 128].reshape(ROWS, 128) for t in PAIRS[j]]
+        return jnp.concatenate(tiles, axis=1)
 
     def rows_of(ref, half):
         return ref[half].reshape(ROWS, WIDTH)
@@ -173,26 +195,26 @@
             {"seq": mate, "dp": d},
         )
 
-    def grad_terms(tap, terms, add, send):
-        def body(j, carry):
-            cols = cols_of(j)
-            total = dot(at_v[terms[0][0]], cots(terms[0][1], terms[0][2], cols))
+    def grad_terms(tap, terms, add, send, tiles=range(TILES)):
+        for j in tiles:
+            total = dot(at_v[terms[0][0]], cots(terms[0][1], terms[0][2], j))
             for act_half, ref, half in terms[1:]:
-                total = total + dot(at_v[act_half], cots(ref, half, cols))
+                total = total + dot(at_v[act_half], cots(ref, half, j))
             total = total.reshape(4, 4, 2, 24, TILE)
             if add:
                 total = total + part[tap, j]
             part[tap, j] = total
             if send:
                 core_copy(tap, j).start()
-            return carry
-
-        lax.fori_loop(0, TILES, body, 0)
-
-    def y_copy(tap):
+
+    def y_copy(tap, chunk):
+        rows = pl.ds(64 * chunk, 64 - 32 * chunk)
         return [
-        remote(ys.at[lax.rem(y + k, 4), tap], yr.at[k - 1, tap], y_s.at[tap, k - 1], y_r.at[tap, k - 1], y_partner(k))
-        for k in range(1, 4)
+            remote(
+                ys.at[lax.rem(y + k, 4), tap, :, rows], yr.at[k - 1, tap, :, rows],
+                y_s.at[tap, chunk, k - 1], y_r.at[tap, chunk, k - 1], y_partner(k),
+            )
+            for k in range(1, 4)
         ]
 
     def x_copy(tap):
@@ -208,9 +230,13 @@
         ]
 
 
-    def x_first(tap):
+    def x_first(tap, chunk):
+        cols = pl.ds(512 * chunk, 512 - 256 * chunk)
         return [
-            remote(xs2.at[lax.rem(x + k, 4), tap], xr2.at[k - 1, tap], x2_s.at[tap, k - 1], x2_r.at[tap, k - 1], x_partner(k))
+            remote(
+                xs2.at[lax.rem(x + k, 4), tap, :, cols], xr2.at[k - 1, tap, :, cols],
+                x2_s.at[tap, chunk, k - 1], x2_r.at[tap, chunk, k - 1], x_partner(k),
+            )
             for k in range(1, 4)
         ]
 
@@ -224,48 +250,43 @@
     lane32 = lax.broadcasted_iota(jnp.int32, (32, 128), 1)
     lane96 = lax.broadcasted_iota(jnp.int32, (96, 128), 1)
 
-    def columns_for(to, tiles, lane):
-        full = tiles[FULL_TILE[to]]
-        shared = tiles[SHARED_TILE[to]]
+    def packed_for(to, shared, lane):
         a, b = shared[: lane.shape[0]], shared[lane.shape[0] :]
         if to % 2 == 0:
-            return full, jnp.where(lane < 64, a, pltpu.roll(b, 64, 1))
-        return full, jnp.where(lane < 64, pltpu.roll(a, 64, 1), b)
-
-    def receive_core(tap):
-        for j in range(TILES):
-            core_copy(tap, j).wait_recv()
-
-    def send_y(tap):
+            return jnp.where(lane < 64, a, pltpu.roll(b, 64, 1))
+        return jnp.where(lane < 64, pltpu.roll(a, 64, 1), b)
+
+    def send_y(tap, chunk):
         def body(i, carry):
-            tiles = []
-            for j in range(TILES):
+            for j in CHUNKS[chunk]:
                 total = part[tap, j, :, i, core, :16] + mate_part[tap, j, :, i, :16]
                 total = total.reshape(64, TILE)
-                tiles += [total[:, :128], total[:, 128:]]
-            for to in range(4):
-                full, packed = columns_for(to, tiles, lane32)
-                ys[to, tap, i, :64] = full.astype(BF16)
-                ys[to, tap, i, 64:] = packed.astype(BF16)
+                tiles = total[:, :128], total[:, 128:]
+                if chunk == 0:
+                    for half in range(2):
+                        ys[2 * j + half, tap, i, :64] = tiles[half].astype(BF16)
+                else:
+                    for to in range(4):
+                        ys[to, tap, i, 64:] = packed_for(to, tiles[to // 2], lane32).astype(BF16)
             return carry
 
         lax.fori_loop(0, 4, body, 0)
-        for copy in y_copy(tap):
+        for copy in y_copy(tap, chunk):
             copy.start()
 
-    def send_x_first(tap):
+    def send_x_first(tap, chunk):
         def body(i, carry):
-            for j in range(TILES):
+            for j in CHUNKS[chunk]:
                 total = part[tap, j, :, i, core, 16:] + mate_part[tap, j, :, i, 16:]
                 xs2[i, tap, :, j * TILE : (j + 1) * TILE] = total.reshape(32, TILE).astype(BF16)
             return carry
 
         lax.fori_loop(0, 4, body, 0)
-        for copy in x_first(tap):
+        for copy in x_first(tap, chunk):
             copy.start()
 
     def send_y_second(tap):
-        for copy in x_first(tap):
+        for copy in x_first(tap, 0) + x_first(tap, 1):
             copy.wait_recv()
         tiles = []
         for j in range(6):
@@ -275,19 +296,19 @@
                 total = total + xr2[k, tap, :, cols].astype(F32)
             tiles.append(total)
         for to in range(4):
-            full, packed = columns_for(to, tiles, lane16)
-            ys2[to, tap, :32] = full.astype(BF16)
-            ys2[to, tap, 32:] = packed.astype(BF16)
+            ys2[to, tap, :32] = tiles[to].astype(BF16)
+            ys2[to, tap, 32:] = packed_for(to, tiles[4 + to // 2], lane16).astype(BF16)
         for copy in y_second(tap):
             copy.start()
 
-    def send_first(tap):
-        receive_core(tap)
-        send_y(tap)
-        send_x_first(tap)
+    def send_first(tap, chunk):
+        for j in CHUNKS[chunk]:
+            core_copy(tap, j).wait_recv()
+        send_y(tap, chunk)
+        send_x_first(tap, chunk)
 
     def send_x(tap):
-        for copy in y_copy(tap):
+        for copy in y_copy(tap, 0) + y_copy(tap, 1):
             copy.wait_recv()
 
         def body(i, carry):
@@ -366,41 +387,43 @@
 
     early, late = 2 * core, 2 - 2 * core
 
-    def grad_outer(tap, half):
-        grad_terms(tap, [(half, c_halo, half)], True, True)
-
-    loads[2].wait()
-    loads[3].wait()
+    def grad_outer(tap, half, chunk):
+        grad_terms(tap, [(half, c_halo, half)], True, True, CHUNKS[chunk])
+
     grad_terms(1, [(0, c_v, 0), (1, c_v, 1)], False, True)
     grad_terms(0, [(0, c_v, 1)], False, False)
-    send_first(1)
     grad_terms(2, [(1, c_v, 0)], False, False)
-    receive_early(0, c_halo)
-    grad_outer(early, 1 - core)
+    send_first(1, 0)
+    send_first(1, 1)
+    for chunk in range(2):
+        receive_early(c_halo, cot_parts[chunk])
+        grad_outer(early, 1 - core, chunk)
     loads[4].wait()
-    lax.fori_loop(0, 1, back_inner, 0)
-    receive_late(0, c_halo)
-    grad_outer(late, core)
-    send_first(late)
-    send_first(early)
-    start_halo(act_halo)
+    for chunk in range(2):
+        receive_late(c_halo, cot_parts[chunk])
+        if chunk == 1:
+            start_halo(act_halo[0])
+        grad_outer(late, core, chunk)
+        send_first(late, chunk)
+        send_first(early, chunk)
     send_x(1)
     send_y_second(1)
-    lax.fori_loop(1, TILES, back_inner, 0)
+    lax.fori_loop(0, TILES, back_inner, 0)
     lax.fori_loop(0, 48, derive, 0, unroll=2)
-    send_z(1)
     send_x(late)
     send_y_second(late)
+    send_x(early)
+    send_y_second(early)
+    start_halo(act_halo[1])
+    send_z(1)
     lax.fori_loop(0, TILES, back_outer, 0)
     store(0, g_v, gin_hbm)
-    send_x(early)
-    send_y_second(early)
-    lax.fori_loop(0, 2, conv_inner, 0)
     send_z(late)
     send_z(early)
-    lax.fori_loop(2, TILES, conv_inner, 0)
-    receive_early(1, a_halo)
-    receive_late(1, a_halo)
+    lax.fori_loop(0, TILES, conv_inner, 0)
+    for parts in act_parts:
+        receive_early(a_halo, parts)
+        receive_late(a_halo, parts)
     lax.fori_loop(0, TILES, conv_outer, 0)
     store(1, o_v, out_hbm)
     for tap in (1, late, early):
@@ -411,12 +434,15 @@
             total = total + zr[k, tap]
         wg_ref[tap] = (total * FACTOR)[:, :96]
 
-    sent_halo(cot_halo)
-    sent_halo(act_halo)
+    for chunk in cot_halo + act_halo:
+        for copies in chunk:
+            sent_halo(copies)
     for tap in range(3):
         for j in range(TILES):
             core_copy(tap, j).wait_send()
-        for copy in y_copy(tap) + x_copy(tap) + z_copy(tap) + x_first(tap) + y_second(tap):
+        for copy in y_copy(tap, 0) + y_copy(tap, 1) + x_first(tap, 0) + x_first(tap, 1):
+            copy.wait_send()
+        for copy in x_copy(tap) + z_copy(tap) + y_second(tap):
             copy.wait_send()
     for pending in stores:
         pending.wait()
@@ -458,9 +484,9 @@
             vmem((3, 3, 32, WIDTH), BF16),
             vmem((4, 3, 48, 128), BF16),
             vmem((3, 3, 48, 128), BF16),
-            dma((5,)), dma((4,)), dma((4,)), dma((4,)), dma((3, 3)), dma((3, 3)),
-            dma((3, 3)), dma((3, 3)), dma((3, 3)), dma((3, 3)), dma((3, 7)), dma((3, 7)),
-            dma((3, 3)), dma((3, 3)), dma((3, 3)), dma((3, 3)),
+            dma((5,)), dma((4,)), dma((10 + 2 * len(PIECES),)), dma((10 + 2 * len(PIECES),)),
+            dma((3, 3)), dma((3, 3)), dma((3, 2, 3)), dma((3, 2, 3)), dma((3, 3)), dma((3, 3)), dma((3, 7)), dma((3, 7)),
+            dma((3, 3)), dma((3, 3)), dma((3, 2, 3)), dma((3, 2, 3)),
         ],
         compiler_params=pltpu.CompilerParams(
             collective_id=0, has_side_effects=True, vmem_limit_bytes=50 * 1024 * 1024

time: 55.3 us -> 50.8 us (0.919)
  Pallas kernels: 51.7 us -> 47.2 us
    pallas_call x1, Pallas kernels: 51.7 us -> 47.2 us  [on_device(): pl.pallas_call(kernel, out_shape=(block, block, jax.ShapeDtypeStruct((3,...]
where the time goes in v3:
time: 50.8 us
  Pallas kernels  47.2 us (93%)
  local copies, waits for them, and re-layouts  2.9 us (6%)
  between operations  0.64 us (1%)
    pallas_call x1, Pallas kernels, on_device(): pl.pallas_call(kernel, out_shape=(block, block, jax.ShapeDtypeStruct((3,...  47.2 us
    unnamed x3, local copies, waits for them, and re-layouts  2.9 us

profile of v3, /device:TPU:1, one launch (start us, length us, event | category | flops | bytes accessed | tf_op | source)
XLA Modules:
  0.0 50.8 jit_solution(1644907636310668822)
XLA Ops:
  0.6 47.2 %shard_map.58 = (bf16[8,128,768]{2,1,0:T(8,128)(2,1)S(1)}, bf16[8,128,768]{2,1,0:T(8,128)(2,1)S(1)}, f32[3,24,96]{2,1,0:T(8,128)S(1)}) custom-call(bf16[8,128,768]{2,1,0:T(8,128)(2,1)} %f_hbm.1, bf16[3,768,768]{2,1,0:T(8,128)(2,1)} %k_hbm.1, bf16[8,128,768]{2,1,0:T(8,128)(2,1)} %c_hbm.1), custom_call_target="tpu_custom_call" | custom-call | flops 10871635968 | bytes 10485760 | tf_op jit(solution)/shard_map/pallas_call | solution.py:457
  47.9 1.1 %copy.9 = bf16[8,128,768]{2,1,0:T(8,128)(2,1)} copy(bf16[8,128,768]{2,1,0:T(8,128)(2,1)S(1)} %get-tuple-element.6) | data formatting | bytes 3145728
  49.0 1.1 %copy.10 = bf16[8,128,768]{2,1,0:T(8,128)(2,1)} copy(bf16[8,128,768]{2,1,0:T(8,128)(2,1)S(1)} %get-tuple-element.7) | data formatting | bytes 3145728
  50.1 0.6 %copy.11 = f32[3,24,96]{2,1,0:T(8,128)} copy(f32[3,24,96]{2,1,0:T(8,128)S(1)} %get-tuple-element.8) | data formatting | bytes 55296

commit v4 on v3

--- a/solution.py
+++ b/solution.py
@@ -426,14 +426,6 @@
         receive_late(a_halo, parts)
     lax.fori_loop(0, TILES, conv_outer, 0)
     store(1, o_v, out_hbm)
-    for tap in (1, late, early):
-        for copy in z_copy(tap):
-            copy.wait_recv()
-        total = zs[z, tap]
-        for k in range(7):
-            total = total + zr[k, tap]
-        wg_ref[tap] = (total * FACTOR)[:, :96]
-
     for chunk in cot_halo + act_halo:
         for copies in chunk:
             sent_halo(copies)
@@ -442,7 +434,18 @@
             core_copy(tap, j).wait_send()
         for copy in y_copy(tap, 0) + y_copy(tap, 1) + x_first(tap, 0) + x_first(tap, 1):
             copy.wait_send()
-        for copy in x_copy(tap) + z_copy(tap) + y_second(tap):
+        for copy in x_copy(tap) + y_second(tap):
+            copy.wait_send()
+    for tap in (1, late, early):
+        for copy in z_copy(tap):
+            copy.wait_recv()
+        total = zs[z, tap]
+        for k in range(7):
+            total = total + zr[k, tap]
+        wg_ref[tap] = (total * FACTOR)[:, :96]
+
+    for tap in range(3):
+        for copy in z_copy(tap):
             copy.wait_send()
     for pending in stores:
         pending.wait()

time: 50.8 us -> 50.7 us (level)
  no operation moved by 1% of the time
where the time goes in v4:
time: 50.7 us; the launch traced here: 50.6 us
  Pallas kernels  47.1 us (93%)
  local copies, waits for them, and re-layouts  2.9 us (6%)
  between operations  0.64 us (1%)
    pallas_call x1, Pallas kernels, on_device(): pl.pallas_call(kernel, out_shape=(block, block, jax.ShapeDtypeStruct((3,...  47.1 us
    unnamed x3, local copies, waits for them, and re-layouts  2.9 us

profile of v4, /device:TPU:1, one launch (start us, length us, event | category | flops | bytes accessed | tf_op | source)
XLA Modules:
  0.0 50.6 jit_solution(7689996074248854911)
XLA Ops:
  0.6 47.1 %shard_map.58 = (bf16[8,128,768]{2,1,0:T(8,128)(2,1)S(1)}, bf16[8,128,768]{2,1,0:T(8,128)(2,1)S(1)}, f32[3,24,96]{2,1,0:T(8,128)S(1)}) custom-call(bf16[8,128,768]{2,1,0:T(8,128)(2,1)} %f_hbm.1, bf16[3,768,768]{2,1,0:T(8,128)(2,1)} %k_hbm.1, bf16[8,128,768]{2,1,0:T(8,128)(2,1)} %c_hbm.1), custom_call_target="tpu_custom_call" | custom-call | flops 10871635968 | bytes 10485760 | tf_op jit(solution)/shard_map/pallas_call | solution.py:460
  47.7 1.1 %copy.9 = bf16[8,128,768]{2,1,0:T(8,128)(2,1)} copy(bf16[8,128,768]{2,1,0:T(8,128)(2,1)S(1)} %get-tuple-element.6) | data formatting | bytes 3145728
  48.9 1.1 %copy.10 = bf16[8,128,768]{2,1,0:T(8,128)(2,1)} copy(bf16[8,128,768]{2,1,0:T(8,128)(2,1)S(1)} %get-tuple-element.7) | data formatting | bytes 3145728
  50.0 0.6 %copy.11 = f32[3,24,96]{2,1,0:T(8,128)} copy(f32[3,24,96]{2,1,0:T(8,128)S(1)} %get-tuple-element.8) | data formatting | bytes 55296
